TPU v7x, 32 devices: a whole 2x2x4 slice. The times are simulated.
32 devices in a mesh: ctx: 8 (over y, x, core), ch: 4 (over z).
Axes of the slice: x: 2, y: 2, z: 4, core: 2. Of those that a mesh axis runs over, the one named last changes fastest.
Arguments:
- proj: bfloat16 [3, 4096, 2048], P(None, 'ch', 'ctx'), may hold values from -6 to 6
- short_filter: float32 [3, 4096, 3], P(None, 'ch'), may hold values from -3 to 3
- residues: float32 [4096, 16], P('ch'), may hold values from -1.8 to 1.8
- decays: float32 [4096, 16], P('ch'), may hold values from 0.00024414062 to 0.03
- skip: float32 [4096], P('ch'), may hold values from -1 to 1
- w_out: bfloat16 [4096, 4096], P(None, 'ch'), may hold values from -0.09375 to 0.09375
Outputs:
- mixed_out: bfloat16 [2048, 4096], P('ctx', 'ch')
All inputs are finite; a program needn't handle non-finite values.
Results may differ from a plain program's by a relative error of at most 0.015.
Values may be sent and summed in bfloat16 or wider, within the bound.
A program may use at most 192 MiB of HBM per device.

v0:
```python
import functools

import jax
import jax.numpy as jnp
from jax import lax
from jax.experimental import pallas as pl
from jax.experimental.pallas import tpu as pltpu
from jax.sharding import PartitionSpec as P

MESH = pl.DeviceIdType.MESH
LANES = 128


def rounded(value):
    return value.astype(jnp.bfloat16).astype(jnp.float32)


def fused_kernel(
    dims, proj_hbm, short_hbm, weight_hbm, rate_hbm, skip_hbm, w_hbm, out_ref,
    proj_v, short_v, weight_v, rate_v, skip_v, coef_ref, w_v, mixed, signal, gate_rows, states, gathered, total,
    in_sem, halo_send, halo_recv, state_send, state_recv, send_sem, recv_sem,
):
    n_ctx, n_ch, length, groups, modes, halo, parts = dims
    width = groups * LANES
    rows = length // parts
    ctx = lax.axis_index("ctx")
    ch = lax.axis_index("ch")

    small = [
        pltpu.make_async_copy(source, target, in_sem.at[2 + k])
        for k, (source, target) in enumerate(
            [(rate_hbm, rate_v), (weight_hbm, weight_v), (short_hbm, short_v), (skip_hbm, skip_v)]
        )
    ]
    for copy in small:
        copy.start()
    load_proj = pltpu.make_async_copy(proj_hbm, proj_v, in_sem.at[0])
    load_proj.start()
    load_w = pltpu.make_async_copy(w_hbm, w_v, in_sem.at[1])
    load_w.start()

    barrier = pltpu.get_barrier_semaphore()

    def greet(step, carry):
        pl.semaphore_signal(
            barrier, inc=1, device_id={"ctx": lax.rem(ctx + step, n_ctx)}, device_id_type=MESH
        )
        return carry

    lax.fori_loop(1, n_ctx, greet, 0)

    @pl.when(ch > 0)
    def _():
        pl.semaphore_signal(barrier, inc=1, device_id={"ch": ch - 1}, device_id_type=MESH)

    @pl.when(ch < n_ch - 1)
    def _():
        pl.semaphore_signal(barrier, inc=1, device_id={"ch": ch + 1}, device_id_type=MESH)

    inner = jnp.where(ch > 0, 1, 0) + jnp.where(ch < n_ch - 1, 1, 0)

    for copy in small:
        copy.wait()

    def spread(base, value):
        for group in range(groups):
            coef_ref[pl.ds(base * groups + group, value.shape[0], stride=groups), :] = (
                value[:, group * LANES:(group + 1) * LANES]
            )

    rate = rate_v[...]
    spread(0, jnp.exp(-rate))
    spread(modes, weight_v[...] * jnp.sqrt(jnp.tanh(rate) * (1.0 + jnp.exp(-2.0 * rate))))
    spread(2 * modes, jnp.exp(-float(length) * rate))
    spread(3 * modes, jnp.exp(-float(length - 2) * rate))
    for i in range(3):
        spread(4 * modes + 3 * i, short_v[i])
    spread(4 * modes + 9, skip_v[...])

    def coef(index):
        return coef_ref[index * groups:(index + 1) * groups, :]

    decay = [coef(m) for m in range(modes)]
    taps = [[coef(4 * modes + 3 * i + m) for m in range(3)] for i in range(3)]
    skip = coef(4 * modes + 9)

    load_proj.wait()
    row_ids = lax.broadcasted_iota(jnp.int32, (length, length), 0)
    col_ids = lax.broadcasted_iota(jnp.int32, (length, length), 1)
    eye = jnp.where(row_ids == col_ids, 1.0, 0.0).astype(jnp.bfloat16)
    wide = min(width, 256)
    for i in range(3):
        for part in range(width // wide):
            turned = lax.dot_general(
                eye, proj_v[i, part * wide:(part + 1) * wide, :],
                (((1,), (1,)), ((), ())), preferred_element_type=jnp.float32,
            )
            for j in range(wide // LANES):
                group = part * (wide // LANES) + j
                mixed[i, pl.ds(halo * groups + group, length, stride=groups), :] = (
                    turned[:, j * LANES:(j + 1) * LANES]
                )

    pl.semaphore_wait(barrier, n_ctx - 1 + inner)

    edge = halo * groups
    halo_copy = pltpu.make_async_remote_copy(
        src_ref=mixed.at[:, pl.ds(length * groups, edge), :],
        dst_ref=mixed.at[:, pl.ds(0, edge), :],
        send_sem=halo_send.at[0],
        recv_sem=halo_recv.at[0],
        device_id={"ctx": lax.rem(ctx + 1, n_ctx)},
        device_id_type=MESH,
    )

    @pl.when(ctx < n_ctx - 1)
    def _():
        halo_copy.start()

    @pl.when(ctx == 0)
    def _():
        mixed[:, pl.ds(0, edge), :] = jnp.zeros((3, edge, LANES), jnp.float32)

    def short(i, t):
        def at(back):
            start = (t + halo - back) * groups
            if not isinstance(start, int):
                start = pl.multiple_of(start, groups)
            return mixed[i, pl.ds(start, groups), :]

        return taps[i][0] * at(0) + taps[i][1] * at(1) + taps[i][2] * at(2)

    def row_of(t):
        start = t * groups
        if not isinstance(start, int):
            start = pl.multiple_of(start, groups)
        return pl.ds(start, groups)

    def absorb(t, state):
        value = rounded(short(1, t) * short(2, t))
        signal[row_of(t), :] = value
        return tuple(d * s + value for d, s in zip(decay, state))

    empty = tuple(jnp.zeros((groups, LANES), jnp.float32) for _ in range(modes))
    state = lax.fori_loop(2, length, absorb, empty, unroll=2)

    @pl.when(ctx > 0)
    def _():
        halo_copy.wait_recv()

    first = rounded(short(1, 0) * short(2, 0))
    second = rounded(short(1, 1) * short(2, 1))
    signal[row_of(0), :] = first
    signal[row_of(1), :] = second
    for m in range(modes):
        own = state[m] + coef(3 * modes + m) * (decay[m] * first + second)
        states[ctx, m * groups:(m + 1) * groups, :] = own

    def state_copy(source, target):
        return pltpu.make_async_remote_copy(
            src_ref=states.at[source],
            dst_ref=states.at[source],
            send_sem=state_send.at[target],
            recv_sem=state_recv.at[source],
            device_id={"ctx": target},
            device_id_type=MESH,
        )

    def send_state(target, carry):
        state_copy(ctx, target).start()
        return carry

    lax.fori_loop(ctx + 1, n_ctx, send_state, 0)

    def take_state(source, carried):
        state_copy(source, ctx).wait_recv()
        return tuple(
            coef(2 * modes + m) * carried[m] + states[source, m * groups:(m + 1) * groups, :]
            for m in range(modes)
        )

    state = lax.fori_loop(0, ctx, take_state, empty)

    gain = [coef(modes + m) for m in range(modes)]

    def advance(t, state):
        value = signal[row_of(t), :]
        state = tuple(d * s + value for d, s in zip(decay, state))
        terms = [g * s for g, s in zip(gain, state)]
        while len(terms) > 1:
            terms = [sum(terms[k:k + 2][1:], terms[k]) for k in range(0, len(terms), 2)]
        gate_rows[row_of(t), :] = rounded(short(0, t)) * (rounded(terms[0]) + skip * value)
        return state

    def block_copy(block, part, side):
        window = gathered.at[block, pl.ds(pl.multiple_of(part * rows, rows), rows), :]
        return pltpu.make_async_remote_copy(
            src_ref=window,
            dst_ref=window,
            send_sem=send_sem.at[side, block, part],
            recv_sem=recv_sem.at[block, part],
            device_id={"ch": jnp.clip(ch - 1 + 2 * side, 0, n_ch - 1)},
            device_id_type=MESH,
        )

    for part in range(parts):
        state = lax.fori_loop(part * rows, (part + 1) * rows, advance, state, unroll=2)
        for group in range(groups):
            tile = gate_rows[pl.ds(part * rows * groups + group, rows, stride=groups), :]
            gathered[ch, part * rows:(part + 1) * rows, group * LANES:(group + 1) * LANES] = (
                tile.astype(jnp.bfloat16)
            )

        @pl.when(ch > 0)
        def _():
            block_copy(ch, part, 0).start()

        @pl.when(ch < n_ch - 1)
        def _():
            block_copy(ch, part, 1).start()

    load_w.wait()

    def product(block, part):
        lhs = gathered[block, pl.ds(pl.multiple_of(part * rows, rows), rows), :]
        rhs = w_v[pl.ds(pl.multiple_of(block * width, width), width), :]
        return jnp.dot(lhs, rhs, preferred_element_type=jnp.float32)

    def own_part(part, carry):
        total[pl.ds(pl.multiple_of(part * rows, rows), rows), :] = product(ch, part)
        return carry

    lax.fori_loop(0, parts, own_part, 0)

    for distance in range(1, n_ch):
        def one_part(part, carry):
            for side in (0, 1):
                block = ch + distance if side == 0 else ch - distance
                here = block < n_ch if side == 0 else block >= 0
                further = (ch > 0) if side == 0 else (ch < n_ch - 1)

                @pl.when(here)
                def _():
                    block_copy(block, part, side).wait_recv()

                @pl.when(here & further)
                def _():
                    block_copy(block, part, side).start()

                @pl.when(here)
                def _():
                    total[pl.ds(pl.multiple_of(part * rows, rows), rows), :] += product(
                        block, part
                    )
            return carry

        lax.fori_loop(0, parts, one_part, 0)

    out_ref[...] = total[...].astype(jnp.bfloat16)

    @pl.when(ctx < n_ctx - 1)
    def _():
        halo_copy.wait_send()

    def sent_state(target, carry):
        state_copy(ctx, target).wait_send()
        return carry

    lax.fori_loop(ctx + 1, n_ctx, sent_state, 0)

    def sent_left(block, carry):
        for part in range(parts):
            block_copy(block, part, 0).wait_send()
        return carry

    def sent_right(block, carry):
        for part in range(parts):
            block_copy(block, part, 1).wait_send()
        return carry

    @pl.when(ch > 0)
    def _():
        lax.fori_loop(ch, n_ch, sent_left, 0)

    @pl.when(ch < n_ch - 1)
    def _():
        lax.fori_loop(0, ch + 1, sent_right, 0)


def per_device(dims_mesh, proj, short_filter, residues, decays, skip, w_out):
    n_ctx, n_ch = dims_mesh
    _, width, length = proj.shape
    modes = residues.shape[1]
    groups = width // LANES
    halo = max(2, 8 // groups)
    parts = 4
    dims = (n_ctx, n_ch, length, groups, modes, halo, parts)
    features = w_out.shape[1]
    total_width = w_out.shape[0]
    return pl.pallas_call(
        functools.partial(fused_kernel, dims),
        out_shape=jax.ShapeDtypeStruct((length, features), jnp.bfloat16),
        in_specs=[
            pl.BlockSpec(memory_space=pl.ANY),
        ] * 6,
        out_specs=pl.BlockSpec(memory_space=pltpu.VMEM),
        scratch_shapes=[
            pltpu.VMEM(proj.shape, jnp.bfloat16),
            pltpu.VMEM((3, 3, width), jnp.float32),
            pltpu.VMEM((modes, width), jnp.float32),
            pltpu.VMEM((modes, width), jnp.float32),
            pltpu.VMEM((1, width), jnp.float32),
            pltpu.VMEM(((4 * modes + 10) * groups, LANES), jnp.float32),
            pltpu.VMEM(w_out.shape, jnp.bfloat16),
            pltpu.VMEM((3, (length + halo) * groups, LANES), jnp.float32),
            pltpu.VMEM((length * groups, LANES), jnp.float32),
            pltpu.VMEM((length * groups, LANES), jnp.float32),
            pltpu.VMEM((n_ctx, modes * groups, LANES), jnp.float32),
            pltpu.VMEM((n_ch, length, width), jnp.bfloat16),
            pltpu.VMEM((length, features), jnp.float32),
            pltpu.SemaphoreType.DMA((6,)),
            pltpu.SemaphoreType.DMA((1,)),
            pltpu.SemaphoreType.DMA((1,)),
            pltpu.SemaphoreType.DMA((n_ctx,)),
            pltpu.SemaphoreType.DMA((n_ctx,)),
            pltpu.SemaphoreType.DMA((2, n_ch, parts)),
            pltpu.SemaphoreType.DMA((n_ch, parts)),
        ],
        compiler_params=pltpu.CompilerParams(
            collective_id=0, has_side_effects=True, vmem_limit_bytes=63 * 1024 * 1024
        ),
        cost_estimate=pl.CostEstimate(
            flops=2 * length * total_width * features,
            bytes_accessed=2 * (total_width * features + 3 * width * length + length * features),
            transcendentals=0,
        ),
    )(proj, short_filter.transpose(0, 2, 1), residues.T, decays.T, skip[None, :], w_out)


def solution(mesh):
    in_specs = (
        P(None, "ch", "ctx"),
        P(None, "ch", None),
        P("ch", None),
        P("ch", None),
        P("ch"),
        P(None, "ch"),
    )
    dims_mesh = (mesh.shape["ctx"], mesh.shape["ch"])
    return jax.shard_map(
        functools.partial(per_device, dims_mesh),
        mesh=mesh, in_specs=in_specs, out_specs=P("ctx", "ch"), check_vma=False,
    )
```

profile of v0, /device:TPU:5, one launch (start us, length us, event | category | flops | bytes accessed | tf_op | source)
XLA Modules:
  0.0 53.2 jit_solution(12814733702854211573)
XLA Ops:
  0.0 51.3 %shard_map.64 = bf16[256,1024]{1,0:T(8,128)(2,1)} custom-call(bf16[3,1024,256]{2,1,0:T(8,128)(2,1)} %proj_hbm.1, f32[3,3,1024]{2,1,0:T(4,128)} %bitcast.6, f32[16,1024]{1,0:T(8,128)} %bitcast.4, f32[16,1024]{1,0:T(8,128)} %bitcast.5, f32[1,1024]{1,0:T(1,128)} %bitcast.7, bf16[4096,1024]{1,0:T(8,128)(2,1)} %w_hbm.1), custom_call_target="tpu_custom_call" | custom-call | flops 2147483648 | bytes 10485760 | tf_op jit(solution)/shard_map/pallas_call | solution.py:300
  51.3 1.9 %copy.8 = bf16[256,1024]{1,0:T(8,128)(2,1)} copy(bf16[256,1024]{1,0:T(8,128)(2,1)} %shard_map.64) | data formatting | bytes 1048576
where the time goes:
time: 53.3 us; the launch traced here: 53.2 us
  Pallas kernels  51.3 us (96%)
  local copies, waits for them, and re-layouts  1.87 us (4%)
    pallas_call x1, Pallas kernels, per_device(): pl.pallas_call(functools.partial(fused_kernel, dims), out_shape=jax.Shape...  51.3 us
    unnamed x1, local copies, waits for them, and re-layouts  1.87 us

commit v1 on v0

--- a/solution.py
+++ b/solution.py
@@ -20,7 +20,7 @@
     proj_v, short_v, weight_v, rate_v, skip_v, coef_ref, w_v, mixed, signal, gate_rows, states, gathered, total,
     in_sem, halo_send, halo_recv, state_send, state_recv, send_sem, recv_sem,
 ):
-    n_ctx, n_ch, length, groups, modes, halo, parts = dims
+    n_ctx, n_ch, length, groups, modes, halo, parts, features = dims
     width = groups * LANES
     rows = length // parts
     ctx = lax.axis_index("ctx")
@@ -142,7 +142,10 @@
         return tuple(d * s + value for d, s in zip(decay, state))
 
     empty = tuple(jnp.zeros((groups, LANES), jnp.float32) for _ in range(modes))
-    state = lax.fori_loop(2, length, absorb, empty, unroll=2)
+    state = empty
+    for t in range(2, 8):
+        state = absorb(t, state)
+    state = lax.fori_loop(8, length, absorb, state, unroll=8)
 
     @pl.when(ctx > 0)
     def _():
@@ -204,7 +207,7 @@
         )
 
     for part in range(parts):
-        state = lax.fori_loop(part * rows, (part + 1) * rows, advance, state, unroll=2)
+        state = lax.fori_loop(part * rows, (part + 1) * rows, advance, state, unroll=4)
         for group in range(groups):
             tile = gate_rows[pl.ds(part * rows * groups + group, rows, stride=groups), :]
             gathered[ch, part * rows:(part + 1) * rows, group * LANES:(group + 1) * LANES] = (
@@ -221,22 +224,42 @@
 
     load_w.wait()
 
-    def product(block, part):
-        lhs = gathered[block, pl.ds(pl.multiple_of(part * rows, rows), rows), :]
-        rhs = w_v[pl.ds(pl.multiple_of(block * width, width), width), :]
-        return jnp.dot(lhs, rhs, preferred_element_type=jnp.float32)
-
-    def own_part(part, carry):
-        total[pl.ds(pl.multiple_of(part * rows, rows), rows), :] = product(ch, part)
-        return carry
-
-    lax.fori_loop(0, parts, own_part, 0)
+    slabs = min(parts, max(1, features // 256))
+    slab = features // slabs
+
+    def window(part):
+        return pl.ds(pl.multiple_of(part * rows, rows), rows)
+
+    def weight_rows(block):
+        return pl.ds(pl.multiple_of(block * width, width), width)
+
+    def add_columns(block, part, fresh):
+        cols = pl.ds(pl.multiple_of(part * slab, slab), slab)
+        value = jnp.dot(
+            gathered[block], w_v[weight_rows(block), cols], preferred_element_type=jnp.float32
+        )
+        if fresh:
+            total[:, cols] = value
+        else:
+            total[:, cols] += value
+
+    def add_rows(block, part):
+        total[window(part), :] += jnp.dot(
+            gathered[block, window(part), :], w_v[weight_rows(block), :],
+            preferred_element_type=jnp.float32,
+        )
+
+    def block_at(distance, side):
+        if side == 0:
+            return ch + distance, ch + distance < n_ch
+        return ch - distance, ch >= distance
 
     for distance in range(1, n_ch):
-        def one_part(part, carry):
+        last = distance == n_ch - 1
+
+        def arrive(part):
             for side in (0, 1):
-                block = ch + distance if side == 0 else ch - distance
-                here = block < n_ch if side == 0 else block >= 0
+                block, here = block_at(distance, side)
                 further = (ch > 0) if side == 0 else (ch < n_ch - 1)
 
                 @pl.when(here)
@@ -247,14 +270,44 @@
                 def _():
                     block_copy(block, part, side).start()
 
+        def multiply_before(part):
+            if distance == 1:
+                @pl.when(part < slabs)
+                def _():
+                    add_columns(ch, part, True)
+                return
+            for side in (0, 1):
+                block, here = block_at(distance - 1, side)
+
+                @pl.when(here & (part < slabs))
+                def _():
+                    add_columns(block, part, False)
+
+        def multiply_rows(part):
+            for side in (0, 1):
+                block, here = block_at(distance, side)
+
                 @pl.when(here)
                 def _():
-                    total[pl.ds(pl.multiple_of(part * rows, rows), rows), :] += product(
-                        block, part
-                    )
+                    add_rows(block, part)
+
+        def one_part(part, carry):
+            if last and distance > 1:
+                multiply_before(part)
+                arrive(part)
+                multiply_rows(part)
+            else:
+                arrive(part)
+                multiply_before(part)
             return carry
 
+        def last_rows(part, carry):
+            multiply_rows(part)
+            return carry
+
         lax.fori_loop(0, parts, one_part, 0)
+        if last and distance == 1:
+            lax.fori_loop(0, parts, last_rows, 0)
 
     out_ref[...] = total[...].astype(jnp.bfloat16)
 
@@ -294,8 +347,8 @@
     groups = width // LANES
     halo = max(2, 8 // groups)
     parts = 4
-    dims = (n_ctx, n_ch, length, groups, modes, halo, parts)
     features = w_out.shape[1]
+    dims = (n_ctx, n_ch, length, groups, modes, halo, parts, features)
     total_width = w_out.shape[0]
     return pl.pallas_call(
         functools.partial(fused_kernel, dims),
@@ -327,7 +380,7 @@
             pltpu.SemaphoreType.DMA((n_ch, parts)),
         ],
         compiler_params=pltpu.CompilerParams(
-            collective_id=0, has_side_effects=True, vmem_limit_bytes=63 * 1024 * 1024
+            collective_id=0, has_side_effects=True, vmem_limit_bytes=62 * 1024 * 1024 + 640 * 1024
         ),
         cost_estimate=pl.CostEstimate(
             flops=2 * length * total_width * features,

time: 53.3 us -> 52.4 us (0.983)
  Pallas kernels: 51.3 us -> 50.4 us
    pallas_call x1, Pallas kernels: 51.3 us -> 50.4 us  [per_device(): pl.pallas_call(functools.partial(fused_kernel, dims), out_shape=jax.Shape...]
where the time goes in v1:
time: 52.4 us; the launch traced here: 52.3 us
  Pallas kernels  50.4 us (96%)
  local copies, waits for them, and re-layouts  1.87 us (4%)
    pallas_call x1, Pallas kernels, per_device(): pl.pallas_call(functools.partial(fused_kernel, dims), out_shape=jax.Shape...  50.4 us
    unnamed x1, local copies, waits for them, and re-layouts  1.87 us

profile of v1, /device:TPU:5, one launch (start us, length us, event | category | flops | bytes accessed | tf_op | source)
XLA Modules:
  0.0 52.3 jit_solution(5916287029004470551)
XLA Ops:
  0.0 50.4 %shard_map.64 = bf16[256,1024]{1,0:T(8,128)(2,1)} custom-call(bf16[3,1024,256]{2,1,0:T(8,128)(2,1)} %proj_hbm.1, f32[3,3,1024]{2,1,0:T(4,128)} %bitcast.6, f32[16,1024]{1,0:T(8,128)} %bitcast.4, f32[16,1024]{1,0:T(8,128)} %bitcast.5, f32[1,1024]{1,0:T(1,128)} %bitcast.7, bf16[4096,1024]{1,0:T(8,128)(2,1)} %w_hbm.1), custom_call_target="tpu_custom_call" | custom-call | flops 2147483648 | bytes 10485760 | tf_op jit(solution)/shard_map/pallas_call | solution.py:353
  50.4 1.9 %copy.8 = bf16[256,1024]{1,0:T(8,128)(2,1)} copy(bf16[256,1024]{1,0:T(8,128)(2,1)} %shard_map.64) | data formatting | bytes 1048576

commit v2 on v1

--- a/solution.py
+++ b/solution.py
@@ -17,8 +17,9 @@
 
 def fused_kernel(
     dims, proj_hbm, short_hbm, weight_hbm, rate_hbm, skip_hbm, w_hbm, out_ref,
-    proj_v, short_v, weight_v, rate_v, skip_v, coef_ref, w_v, mixed, signal, gate_rows, states, gathered, total,
-    in_sem, halo_send, halo_recv, state_send, state_recv, send_sem, recv_sem,
+    proj_v, short_v, weight_v, rate_v, skip_v, coef_ref, w_v, mixed, signal, query, gate_rows, pair, chips,
+    gathered, total,
+    in_sem, halo_send, halo_recv, pair_send, pair_recv, state_send, state_recv, send_sem, recv_sem,
 ):
     n_ctx, n_ch, length, groups, modes, halo, parts, features = dims
     width = groups * LANES
@@ -89,7 +90,8 @@
     col_ids = lax.broadcasted_iota(jnp.int32, (length, length), 1)
     eye = jnp.where(row_ids == col_ids, 1.0, 0.0).astype(jnp.bfloat16)
     wide = min(width, 256)
-    for i in range(3):
+
+    def turn(i):
         for part in range(width // wide):
             turned = lax.dot_general(
                 eye, proj_v[i, part * wide:(part + 1) * wide, :],
@@ -101,21 +103,26 @@
                     turned[:, j * LANES:(j + 1) * LANES]
                 )
 
+    turn(1)
+    turn(2)
+
     pl.semaphore_wait(barrier, n_ctx - 1 + inner)
 
     edge = halo * groups
-    halo_copy = pltpu.make_async_remote_copy(
-        src_ref=mixed.at[:, pl.ds(length * groups, edge), :],
-        dst_ref=mixed.at[:, pl.ds(0, edge), :],
-        send_sem=halo_send.at[0],
-        recv_sem=halo_recv.at[0],
-        device_id={"ctx": lax.rem(ctx + 1, n_ctx)},
-        device_id_type=MESH,
-    )
+
+    def halo_copy(first, count):
+        return pltpu.make_async_remote_copy(
+            src_ref=mixed.at[first:first + count, pl.ds(length * groups, edge), :],
+            dst_ref=mixed.at[first:first + count, pl.ds(0, edge), :],
+            send_sem=halo_send.at[first],
+            recv_sem=halo_recv.at[first],
+            device_id={"ctx": lax.rem(ctx + 1, n_ctx)},
+            device_id_type=MESH,
+        )
 
     @pl.when(ctx < n_ctx - 1)
     def _():
-        halo_copy.start()
+        halo_copy(1, 2).start()
 
     @pl.when(ctx == 0)
     def _():
@@ -149,50 +156,118 @@
 
     @pl.when(ctx > 0)
     def _():
-        halo_copy.wait_recv()
+        halo_copy(1, 2).wait_recv()
 
     first = rounded(short(1, 0) * short(2, 0))
     second = rounded(short(1, 1) * short(2, 1))
     signal[row_of(0), :] = first
     signal[row_of(1), :] = second
+
+    chip, core = ctx // 2, lax.rem(ctx, 2)
+    half = modes * groups // 2
     for m in range(modes):
         own = state[m] + coef(3 * modes + m) * (decay[m] * first + second)
-        states[ctx, m * groups:(m + 1) * groups, :] = own
-
-    def state_copy(source, target):
+        pair[core, m * groups:(m + 1) * groups, :] = own
+
+    def pair_copy(source):
         return pltpu.make_async_remote_copy(
-            src_ref=states.at[source],
-            dst_ref=states.at[source],
+            src_ref=pair.at[source],
+            dst_ref=pair.at[source],
+            send_sem=pair_send.at[0],
+            recv_sem=pair_recv.at[0],
+            device_id={"ctx": 2 * chip + 1 - core},
+            device_id_type=MESH,
+        )
+
+    pair_copy(core).start()
+    turn(0)
+
+    @pl.when(ctx < n_ctx - 1)
+    def _():
+        halo_copy(0, 1).start()
+
+    pair_copy(1 - core).wait_recv()
+
+    def half_rows(which, base=0):
+        return pl.ds(pl.multiple_of(base + which * half, half), half)
+
+    chips[chip, half_rows(core), :] = (
+        coef_ref[half_rows(core, 2 * modes * groups), :] * pair[0, half_rows(core), :]
+        + pair[1, half_rows(core), :]
+    )
+
+    def chip_copy(source, which, target):
+        window = chips.at[source, half_rows(which), :]
+        return pltpu.make_async_remote_copy(
+            src_ref=window,
+            dst_ref=window,
             send_sem=state_send.at[target],
-            recv_sem=state_recv.at[source],
+            recv_sem=state_recv.at[source, which],
             device_id={"ctx": target},
             device_id_type=MESH,
         )
 
-    def send_state(target, carry):
-        state_copy(ctx, target).start()
+    def send_chip(target, carry):
+        chip_copy(chip, core, target).start()
         return carry
 
-    lax.fori_loop(ctx + 1, n_ctx, send_state, 0)
-
-    def take_state(source, carried):
-        state_copy(source, ctx).wait_recv()
-        return tuple(
-            coef(2 * modes + m) * carried[m] + states[source, m * groups:(m + 1) * groups, :]
-            for m in range(modes)
-        )
-
-    state = lax.fori_loop(0, ctx, take_state, empty)
+    lax.fori_loop(2 * chip + 2, n_ctx, send_chip, 0)
 
     gain = [coef(modes + m) for m in range(modes)]
+
+    def summed(terms):
+        while len(terms) > 1:
+            terms = [sum(terms[k:k + 2][1:], terms[k]) for k in range(0, len(terms), 2)]
+        return terms[0]
 
     def advance(t, state):
         value = signal[row_of(t), :]
         state = tuple(d * s + value for d, s in zip(decay, state))
-        terms = [g * s for g, s in zip(gain, state)]
-        while len(terms) > 1:
-            terms = [sum(terms[k:k + 2][1:], terms[k]) for k in range(0, len(terms), 2)]
-        gate_rows[row_of(t), :] = rounded(short(0, t)) * (rounded(terms[0]) + skip * value)
+        gate_rows[row_of(t), :] = summed([g * s for g, s in zip(gain, state)])
+        return state
+
+    def advance_query(t, state):
+        query[row_of(t), :] = rounded(short(0, t))
+        return advance(t, state)
+
+    state = empty
+    for t in range(2):
+        state = advance(t, state)
+    for t in range(2, 4):
+        state = advance_query(t, state)
+    lax.fori_loop(4, length, advance_query, state, unroll=4)
+
+    @pl.when(ctx > 0)
+    def _():
+        halo_copy(0, 1).wait_recv()
+
+    for t in range(2):
+        query[row_of(t), :] = rounded(short(0, t))
+
+    def take_chip(source, carried):
+        for which in range(2):
+            chip_copy(source, which, ctx).wait_recv()
+        return tuple(
+            coef(2 * modes + m) * (coef(2 * modes + m) * carried[m])
+            + chips[source, m * groups:(m + 1) * groups, :]
+            for m in range(modes)
+        )
+
+    state = lax.fori_loop(0, chip, take_chip, empty)
+    odd = core == 1
+    state = tuple(
+        gain[m] * jnp.where(
+            odd,
+            coef(2 * modes + m) * state[m] + pair[0, m * groups:(m + 1) * groups, :],
+            state[m],
+        )
+        for m in range(modes)
+    )
+
+    def finish(t, state):
+        state = tuple(d * s for d, s in zip(decay, state))
+        conv = rounded(gate_rows[row_of(t), :] + summed(list(state)))
+        gate_rows[row_of(t), :] = query[row_of(t), :] * (conv + skip * signal[row_of(t), :])
         return state
 
     def block_copy(block, part, side):
@@ -207,7 +282,7 @@
         )
 
     for part in range(parts):
-        state = lax.fori_loop(part * rows, (part + 1) * rows, advance, state, unroll=4)
+        state = lax.fori_loop(part * rows, (part + 1) * rows, finish, state, unroll=8)
         for group in range(groups):
             tile = gate_rows[pl.ds(part * rows * groups + group, rows, stride=groups), :]
             gathered[ch, part * rows:(part + 1) * rows, group * LANES:(group + 1) * LANES] = (
@@ -313,13 +388,16 @@
 
     @pl.when(ctx < n_ctx - 1)
     def _():
-        halo_copy.wait_send()
-
-    def sent_state(target, carry):
-        state_copy(ctx, target).wait_send()
+        halo_copy(1, 2).wait_send()
+        halo_copy(0, 1).wait_send()
+
+    pair_copy(core).wait_send()
+
+    def sent_chip(target, carry):
+        chip_copy(chip, core, target).wait_send()
         return carry
 
-    lax.fori_loop(ctx + 1, n_ctx, sent_state, 0)
+    lax.fori_loop(2 * chip + 2, n_ctx, sent_chip, 0)
 
     def sent_left(block, carry):
         for part in range(parts):
@@ -346,7 +424,7 @@
     modes = residues.shape[1]
     groups = width // LANES
     halo = max(2, 8 // groups)
-    parts = 4
+    parts = 8
     features = w_out.shape[1]
     dims = (n_ctx, n_ch, length, groups, modes, halo, parts, features)
     total_width = w_out.shape[0]
@@ -368,19 +446,23 @@
             pltpu.VMEM((3, (length + halo) * groups, LANES), jnp.float32),
             pltpu.VMEM((length * groups, LANES), jnp.float32),
             pltpu.VMEM((length * groups, LANES), jnp.float32),
-            pltpu.VMEM((n_ctx, modes * groups, LANES), jnp.float32),
+            pltpu.VMEM((length * groups, LANES), jnp.float32),
+            pltpu.VMEM((2, modes * groups, LANES), jnp.float32),
+            pltpu.VMEM((n_ctx // 2, modes * groups, LANES), jnp.float32),
             pltpu.VMEM((n_ch, length, width), jnp.bfloat16),
             pltpu.VMEM((length, features), jnp.float32),
             pltpu.SemaphoreType.DMA((6,)),
+            pltpu.SemaphoreType.DMA((2,)),
+            pltpu.SemaphoreType.DMA((2,)),
             pltpu.SemaphoreType.DMA((1,)),
             pltpu.SemaphoreType.DMA((1,)),
             pltpu.SemaphoreType.DMA((n_ctx,)),
-            pltpu.SemaphoreType.DMA((n_ctx,)),
+            pltpu.SemaphoreType.DMA((n_ctx // 2, 2)),
             pltpu.SemaphoreType.DMA((2, n_ch, parts)),
             pltpu.SemaphoreType.DMA((n_ch, parts)),
         ],
         compiler_params=pltpu.CompilerParams(
-            collective_id=0, has_side_effects=True, vmem_limit_bytes=62 * 1024 * 1024 + 640 * 1024
+            collective_id=0, has_side_effects=True, vmem_limit_bytes=52 * 1024 * 1024
         ),
         cost_estimate=pl.CostEstimate(
             flops=2 * length * total_width * features,

time: 52.4 us -> 52.5 us (level); the launches traced: 52.3 us -> 51.5 us
  Pallas kernels: 50.4 us -> 47.6 us
  local copies, waits for them, and re-layouts: 1.87 us -> 3.96 us
    pallas_call x1, Pallas kernels: 50.4 us -> 47.6 us  [per_device(): pl.pallas_call(functools.partial(fused_kernel, dims), out_shape=jax.Shape...]
    unnamed x1 -> x9, local copies, waits for them, and re-layouts: 1.87 us -> 3.96 us
where the time goes in v2:
time: 52.5 us; the launch traced here: 51.5 us
  Pallas kernels  47.6 us (91%)
  local copies, waits for them, and re-layouts  3.96 us (8%)
    pallas_call x1, Pallas kernels, per_device(): pl.pallas_call(functools.partial(fused_kernel, dims), out_shape=jax.Shape...  47.6 us
    unnamed x9, local copies, waits for them, and re-layouts  3.96 us

profile of v2, /device:TPU:5, one launch (start us, length us, event | category | flops | bytes accessed | tf_op | source)
XLA Modules:
  0.0 51.5 jit_solution(13909579695327371289)
XLA Ops:
  0.0 0.0 copy-start
  0.0 0.8 %copy-done = f32[1024,16]{0,1:T(8,128)S(1)} copy-done((f32[1024,16]{0,1:T(8,128)S(1)}, f32[1024,16]{0,1:T(8,128)}, u32[]{:S(2)}) %copy-start) | copy-done | bytes 65560
  0.8 0.0 copy-start.1
  0.8 0.8 %copy-done.1 = f32[1024,16]{0,1:T(8,128)S(1)} copy-done((f32[1024,16]{0,1:T(8,128)S(1)}, f32[1024,16]{0,1:T(8,128)}, u32[]{:S(2)}) %copy-start.1) | copy-done | bytes 65560
  1.7 0.0 copy-start.2
  1.7 0.8 %copy-done.2 = f32[3,1024,3]{1,2,0:T(4,128)S(1)} copy-done((f32[3,1024,3]{1,2,0:T(4,128)S(1)}, f32[3,1024,3]{1,2,0:T(4,128)}, u32[]{:S(2)}) %copy-start.2) | copy-done | bytes 36888
  2.5 0.0 copy-start.3
  2.5 0.7 %copy-done.3 = f32[1024]{0:T(1024)S(1)} copy-done((f32[1024]{0:T(1024)S(1)}, f32[1024]{0:T(1024)}, u32[]{:S(2)}) %copy-start.3) | copy-done | bytes 4120
  3.2 47.6 %shard_map.64 = bf16[256,1024]{1,0:T(8,128)(2,1)S(1)} custom-call(bf16[3,1024,256]{2,1,0:T(8,128)(2,1)} %proj_hbm.1, f32[3,3,1024]{2,1,0:T(4,128)S(1)} %bitcast.6, f32[16,1024]{1,0:T(8,128)S(1)} %bitcast.4, f32[16,1024]{1,0:T(8,128)S(1)} %bitcast.5, f32[1,1024]{1,0:T(1,128)S(1)} %bitcast.7, bf16[4096,1024]{1,0:T(8,128)(2,1)} %w_hbm.1), custom_call_target="tpu_custom_call" | custom-call | flops 2147483648 | bytes 10485760 | tf_op jit(solution)/shard_map/pallas_call | solution.py:431
  50.8 0.8 %copy.8 = bf16[256,1024]{1,0:T(8,128)(2,1)} copy(bf16[256,1024]{1,0:T(8,128)(2,1)S(1)} %shard_map.64) | data formatting | bytes 1048576
Async XLA Ops:
  0.0 0.8 %copy-start = (f32[1024,16]{0,1:T(8,128)S(1)}, f32[1024,16]{0,1:T(8,128)}, u32[]{:S(2)}) copy-start(f32[1024,16]{0,1:T(8,128)} %param.8) | copy-start | bytes 196612
  0.8 0.8 %copy-start.1 = (f32[1024,16]{0,1:T(8,128)S(1)}, f32[1024,16]{0,1:T(8,128)}, u32[]{:S(2)}) copy-start(f32[1024,16]{0,1:T(8,128)} %param.9) | copy-start | bytes 196612
  1.7 0.8 %copy-start.2 = (f32[3,1024,3]{1,2,0:T(4,128)S(1)}, f32[3,1024,3]{1,2,0:T(4,128)}, u32[]{:S(2)}) copy-start(f32[3,1024,3]{1,2,0:T(4,128)} %param.7) | copy-start | bytes 110596
  2.5 0.7 %copy-start.3 = (f32[1024]{0:T(1024)S(1)}, f32[1024]{0:T(1024)}, u32[]{:S(2)}) copy-start(f32[1024]{0:T(1024)} %param.10) | copy-start | bytes 12292

commit v3 on v2

--- a/solution.py
+++ b/solution.py
@@ -213,29 +213,13 @@
 
     lax.fori_loop(2 * chip + 2, n_ctx, send_chip, 0)
 
-    gain = [coef(modes + m) for m in range(modes)]
-
-    def summed(terms):
-        while len(terms) > 1:
-            terms = [sum(terms[k:k + 2][1:], terms[k]) for k in range(0, len(terms), 2)]
-        return terms[0]
-
-    def advance(t, state):
-        value = signal[row_of(t), :]
-        state = tuple(d * s + value for d, s in zip(decay, state))
-        gate_rows[row_of(t), :] = summed([g * s for g, s in zip(gain, state)])
-        return state
-
-    def advance_query(t, state):
+    def project(t, carry):
         query[row_of(t), :] = rounded(short(0, t))
-        return advance(t, state)
-
-    state = empty
-    for t in range(2):
-        state = advance(t, state)
-    for t in range(2, 4):
-        state = advance_query(t, state)
-    lax.fori_loop(4, length, advance_query, state, unroll=4)
+        return carry
+
+    for t in range(2, 8):
+        project(t, 0)
+    lax.fori_loop(8, length, project, 0, unroll=8)
 
     @pl.when(ctx > 0)
     def _():
@@ -256,18 +240,25 @@
     state = lax.fori_loop(0, chip, take_chip, empty)
     odd = core == 1
     state = tuple(
-        gain[m] * jnp.where(
+        jnp.where(
             odd,
             coef(2 * modes + m) * state[m] + pair[0, m * groups:(m + 1) * groups, :],
             state[m],
         )
         for m in range(modes)
     )
+    gain = [coef(modes + m) for m in range(modes)]
+
+    def summed(terms):
+        while len(terms) > 1:
+            terms = [sum(terms[k:k + 2][1:], terms[k]) for k in range(0, len(terms), 2)]
+        return terms[0]
 
     def finish(t, state):
-        state = tuple(d * s for d, s in zip(decay, state))
-        conv = rounded(gate_rows[row_of(t), :] + summed(list(state)))
-        gate_rows[row_of(t), :] = query[row_of(t), :] * (conv + skip * signal[row_of(t), :])
+        value = signal[row_of(t), :]
+        state = tuple(d * s + value for d, s in zip(decay, state))
+        conv = rounded(summed([g * s for g, s in zip(gain, state)]))
+        gate_rows[row_of(t), :] = query[row_of(t), :] * (conv + skip * value)
         return state
 
     def block_copy(block, part, side):
@@ -282,7 +273,7 @@
         )
 
     for part in range(parts):
-        state = lax.fori_loop(part * rows, (part + 1) * rows, finish, state, unroll=8)
+        state = lax.fori_loop(part * rows, (part + 1) * rows, finish, state, unroll=4)
         for group in range(groups):
             tile = gate_rows[pl.ds(part * rows * groups + group, rows, stride=groups), :]
             gathered[ch, part * rows:(part + 1) * rows, group * LANES:(group + 1) * LANES] = (
@@ -462,7 +453,7 @@
             pltpu.SemaphoreType.DMA((n_ch, parts)),
         ],
         compiler_params=pltpu.CompilerParams(
-            collective_id=0, has_side_effects=True, vmem_limit_bytes=52 * 1024 * 1024
+            collective_id=0, has_side_effects=True, vmem_limit_bytes=62 * 1024 * 1024 + 640 * 1024
         ),
         cost_estimate=pl.CostEstimate(
             flops=2 * length * total_width * features,

time: 52.5 us -> 50.5 us (0.962); the launches traced: 51.5 us -> 50.2 us
  local copies, waits for them, and re-layouts: 3.96 us -> 1.87 us
  Pallas kernels: 47.6 us -> 48.3 us
    unnamed x9 -> x1, local copies, waits for them, and re-layouts: 3.96 us -> 1.87 us
    pallas_call x1, Pallas kernels: 47.6 us -> 48.3 us  [per_device(): pl.pallas_call(functools.partial(fused_kernel, dims), out_shape=jax.Shape...]
where the time goes in v3:
time: 50.5 us; the launch traced here: 50.2 us
  Pallas kernels  48.3 us (96%)
  local copies, waits for them, and re-layouts  1.87 us (4%)
    pallas_call x1, Pallas kernels, per_device(): pl.pallas_call(functools.partial(fused_kernel, dims), out_shape=jax.Shape...  48.3 us
    unnamed x1, local copies, waits for them, and re-layouts  1.87 us

profile of v3, /device:TPU:5, one launch (start us, length us, event | category | flops | bytes accessed | tf_op | source)
XLA Modules:
  0.0 50.2 jit_solution(6070879963537386801)
XLA Ops:
  0.0 48.3 %shard_map.64 = bf16[256,1024]{1,0:T(8,128)(2,1)} custom-call(bf16[3,1024,256]{2,1,0:T(8,128)(2,1)} %proj_hbm.1, f32[3,3,1024]{2,1,0:T(4,128)} %bitcast.6, f32[16,1024]{1,0:T(8,128)} %bitcast.4, f32[16,1024]{1,0:T(8,128)} %bitcast.5, f32[1,1024]{1,0:T(1,128)} %bitcast.7, bf16[4096,1024]{1,0:T(8,128)(2,1)} %w_hbm.1), custom_call_target="tpu_custom_call" | custom-call | flops 2147483648 | bytes 10485760 | tf_op jit(solution)/shard_map/pallas_call | solution.py:422
  48.3 1.9 %copy.8 = bf16[256,1024]{1,0:T(8,128)(2,1)} copy(bf16[256,1024]{1,0:T(8,128)(2,1)} %shard_map.64) | data formatting | bytes 1048576

commit v4 on v3

--- a/solution.py
+++ b/solution.py
@@ -18,8 +18,9 @@
 def fused_kernel(
     dims, proj_hbm, short_hbm, weight_hbm, rate_hbm, skip_hbm, w_hbm, out_ref,
     proj_v, short_v, weight_v, rate_v, skip_v, coef_ref, w_v, mixed, signal, query, gate_rows, pair, chips,
-    gathered, total,
+    gathered, total, help_v, partial,
     in_sem, halo_send, halo_recv, pair_send, pair_recv, state_send, state_recv, send_sem, recv_sem,
+    piece_sem, spread_send, spread_recv, partial_send, partial_recv,
 ):
     n_ctx, n_ch, length, groups, modes, halo, parts, features = dims
     width = groups * LANES
@@ -108,6 +109,74 @@
 
     pl.semaphore_wait(barrier, n_ctx - 1 + inner)
 
+    helped = n_ch == 4 and n_ctx == 8
+    cut = parts // 2
+    at_end = (ch == 0) | (ch == n_ch - 1)
+    inside = jnp.logical_not(at_end)
+    piece = 2 * width // n_ctx
+    far = jnp.where(ch < n_ch // 2, 2, 0)
+
+    def piece_window(index, which):
+        return pl.ds(
+            pl.multiple_of(index * piece + which * (piece // 2), piece // 2), piece // 2
+        )
+
+    def piece_copy():
+        return pltpu.make_async_remote_copy(
+            src_ref=w_hbm.at[pl.ds(pl.multiple_of(far * width + ctx * piece, piece), piece), :],
+            dst_ref=help_v.at[pl.ds(pl.multiple_of(ctx * piece, piece), piece), :],
+            send_sem=piece_sem.at[0],
+            recv_sem=piece_sem.at[1],
+            device_id={"ch": jnp.where(ch < n_ch // 2, 1, n_ch - 2)},
+            device_id_type=MESH,
+        )
+
+    def across(index):
+        return index + 2 - 4 * lax.rem(index // 2, 2)
+
+    x_peer = across(ctx)
+    y_peer = ctx + 4 - 8 * (ctx // 4)
+    corner = across(y_peer)
+    core_peer = ctx + 1 - 2 * lax.rem(ctx, 2)
+    peers = (x_peer, y_peer, core_peer)
+
+    def spread_copy(way, index, which):
+        window = help_v.at[piece_window(index, which), :]
+        return pltpu.make_async_remote_copy(
+            src_ref=window,
+            dst_ref=window,
+            send_sem=spread_send.at[way, index, which],
+            recv_sem=spread_recv.at[index, which],
+            device_id={"ctx": peers[way]},
+            device_id_type=MESH,
+        )
+
+    spread_stages = (
+        ((0, ctx, 0), (1, ctx, 1), (2, ctx, 0), (2, ctx, 1)),
+        ((1, ctx, 0), (1, x_peer, 0), (0, ctx, 1), (0, y_peer, 1), (2, x_peer, 0), (2, y_peer, 1)),
+        ((2, y_peer, 0), (2, corner, 0), (2, x_peer, 1), (2, corner, 1)),
+    )
+    spread_waits = (
+        (),
+        ((x_peer, 0), (y_peer, 1)),
+        ((y_peer, 0), (corner, 0), (x_peer, 1), (corner, 1)),
+    )
+
+    def spread_stage(stage):
+        @pl.when(inside)
+        def _():
+            if stage == 0:
+                piece_copy().wait_recv()
+            for index, which in spread_waits[stage]:
+                spread_copy(0, index, which).wait_recv()
+            for way, index, which in spread_stages[stage]:
+                spread_copy(way, index, which).start()
+
+    if helped:
+        @pl.when(at_end)
+        def _():
+            piece_copy().start()
+
     edge = halo * groups
 
     def halo_copy(first, count):
@@ -288,6 +357,9 @@
         def _():
             block_copy(ch, part, 1).start()
 
+        if helped and part == 3:
+            spread_stage(0)
+
     load_w.wait()
 
     slabs = min(parts, max(1, features // 256))
@@ -299,15 +371,16 @@
     def weight_rows(block):
         return pl.ds(pl.multiple_of(block * width, width), width)
 
-    def add_columns(block, part, fresh):
+    def add_columns(block, part, fresh, height):
         cols = pl.ds(pl.multiple_of(part * slab, slab), slab)
         value = jnp.dot(
-            gathered[block], w_v[weight_rows(block), cols], preferred_element_type=jnp.float32
+            gathered[block, :height, :], w_v[weight_rows(block), cols],
+            preferred_element_type=jnp.float32,
         )
         if fresh:
-            total[:, cols] = value
+            total[:height, cols] = value
         else:
-            total[:, cols] += value
+            total[:height, cols] += value
 
     def add_rows(block, part):
         total[window(part), :] += jnp.dot(
@@ -320,13 +393,55 @@
             return ch + distance, ch + distance < n_ch
         return ch - distance, ch >= distance
 
+    def arriving(distance, side, part):
+        block, here = block_at(distance, side)
+        if helped and distance > 1:
+            here = here & (inside | (part < cut))
+        return block, here
+
+    def partial_copy(piece_at):
+        span = length // 4
+        window_at = partial.at[piece_at * span:(piece_at + 1) * span, :]
+        return pltpu.make_async_remote_copy(
+            src_ref=window_at,
+            dst_ref=window_at,
+            send_sem=partial_send.at[piece_at],
+            recv_sem=partial_recv.at[piece_at],
+            device_id={"ch": jnp.where(ch < n_ch // 2, 0, n_ch - 1)},
+            device_id_type=MESH,
+        )
+
+    def send_partial(piece_at):
+        span = length // 4
+        first = length // 2 + piece_at * span
+
+        @pl.when(inside)
+        def _():
+            if piece_at == 0:
+                for index in (ctx, x_peer, y_peer, corner):
+                    other = index + 1 - 2 * lax.rem(index, 2)
+                    for which in range(2):
+                        spread_copy(2, other, which).wait_recv()
+            value = jnp.dot(
+                gathered[far, first:first + span, :], help_v[:width, :],
+                preferred_element_type=jnp.float32,
+            ) + jnp.dot(
+                gathered[far + 1, first:first + span, :], help_v[width:, :],
+                preferred_element_type=jnp.float32,
+            )
+            partial[piece_at * span:(piece_at + 1) * span, :] = value.astype(jnp.bfloat16)
+            partial_copy(piece_at).start()
+
     for distance in range(1, n_ch):
         last = distance == n_ch - 1
 
         def arrive(part):
             for side in (0, 1):
-                block, here = block_at(distance, side)
+                block, here = arriving(distance, side, part)
                 further = (ch > 0) if side == 0 else (ch < n_ch - 1)
+                if helped:
+                    beyond = (ch > 1) if side == 0 else (ch < n_ch - 2)
+                    further = further & (beyond | (part < cut))
 
                 @pl.when(here)
                 def _():
@@ -340,18 +455,26 @@
             if distance == 1:
                 @pl.when(part < slabs)
                 def _():
-                    add_columns(ch, part, True)
+                    add_columns(ch, part, True, length)
                 return
             for side in (0, 1):
                 block, here = block_at(distance - 1, side)
-
-                @pl.when(here & (part < slabs))
-                def _():
-                    add_columns(block, part, False)
+                if helped and distance > 2:
+                    @pl.when(here & inside & (part < slabs))
+                    def _():
+                        add_columns(block, part, False, length)
+
+                    @pl.when(here & at_end & (part < slabs))
+                    def _():
+                        add_columns(block, part, False, length // 2)
+                else:
+                    @pl.when(here & (part < slabs))
+                    def _():
+                        add_columns(block, part, False, length)
 
         def multiply_rows(part):
             for side in (0, 1):
-                block, here = block_at(distance, side)
+                block, here = arriving(distance, side, part)
 
                 @pl.when(here)
                 def _():
@@ -371,9 +494,32 @@
             multiply_rows(part)
             return carry
 
-        lax.fori_loop(0, parts, one_part, 0)
+        if helped and distance == 1:
+            lax.fori_loop(0, parts - 2, one_part, 0)
+            spread_stage(1)
+            lax.fori_loop(parts - 2, parts, one_part, 0)
+        elif helped and distance == 2:
+            lax.fori_loop(0, cut, one_part, 0)
+            spread_stage(2)
+            lax.fori_loop(cut, parts - 2, one_part, 0)
+            send_partial(0)
+            lax.fori_loop(parts - 2, parts, one_part, 0)
+            send_partial(1)
+        else:
+            lax.fori_loop(0, parts, one_part, 0)
         if last and distance == 1:
             lax.fori_loop(0, parts, last_rows, 0)
+
+    if helped:
+        @pl.when(at_end)
+        def _():
+            span = length // 4
+            for piece_at in range(2):
+                partial_copy(piece_at).wait_recv()
+                first = length // 2 + piece_at * span
+                total[first:first + span, :] += partial[
+                    piece_at * span:(piece_at + 1) * span, :
+                ].astype(jnp.float32)
 
     out_ref[...] = total[...].astype(jnp.bfloat16)
 
@@ -390,23 +536,41 @@
 
     lax.fori_loop(2 * chip + 2, n_ctx, sent_chip, 0)
 
-    def sent_left(block, carry):
-        for part in range(parts):
-            block_copy(block, part, 0).wait_send()
-        return carry
-
-    def sent_right(block, carry):
-        for part in range(parts):
-            block_copy(block, part, 1).wait_send()
-        return carry
+    def sent(side):
+        end_next = (ch == 1) if side == 0 else (ch == n_ch - 2)
+
+        def sent_block(block, carry):
+            for part in range(parts):
+                if helped and part >= cut:
+                    @pl.when((block == ch) | jnp.logical_not(end_next))
+                    def _():
+                        block_copy(block, part, side).wait_send()
+                else:
+                    block_copy(block, part, side).wait_send()
+            return carry
+
+        return sent_block
 
     @pl.when(ch > 0)
     def _():
-        lax.fori_loop(ch, n_ch, sent_left, 0)
+        lax.fori_loop(ch, n_ch, sent(0), 0)
 
     @pl.when(ch < n_ch - 1)
     def _():
-        lax.fori_loop(0, ch + 1, sent_right, 0)
+        lax.fori_loop(0, ch + 1, sent(1), 0)
+
+    if helped:
+        @pl.when(at_end)
+        def _():
+            piece_copy().wait_send()
+
+        @pl.when(inside)
+        def _():
+            for stage in spread_stages:
+                for way, index, which in stage:
+                    spread_copy(way, index, which).wait_send()
+            for piece_at in range(2):
+                partial_copy(piece_at).wait_send()
 
 
 def per_device(dims_mesh, proj, short_filter, residues, decays, skip, w_out):
@@ -442,6 +606,8 @@
             pltpu.VMEM((n_ctx // 2, modes * groups, LANES), jnp.float32),
             pltpu.VMEM((n_ch, length, width), jnp.bfloat16),
             pltpu.VMEM((length, features), jnp.float32),
+            pltpu.VMEM((2 * width, features), jnp.bfloat16),
+            pltpu.VMEM((length // 2, features), jnp.bfloat16),
             pltpu.SemaphoreType.DMA((6,)),
             pltpu.SemaphoreType.DMA((2,)),
             pltpu.SemaphoreType.DMA((2,)),
@@ -451,6 +617,11 @@
             pltpu.SemaphoreType.DMA((n_ctx // 2, 2)),
             pltpu.SemaphoreType.DMA((2, n_ch, parts)),
             pltpu.SemaphoreType.DMA((n_ch, parts)),
+            pltpu.SemaphoreType.DMA((2,)),
+            pltpu.SemaphoreType.DMA((3, n_ctx, 2)),
+            pltpu.SemaphoreType.DMA((n_ctx, 2)),
+            pltpu.SemaphoreType.DMA((2,)),
+            pltpu.SemaphoreType.DMA((2,)),
         ],
         compiler_params=pltpu.CompilerParams(
             collective_id=0, has_side_effects=True, vmem_limit_bytes=62 * 1024 * 1024 + 640 * 1024

time: 50.5 us -> 51.2 us (1.014)
  Pallas kernels: 48.3 us -> 48.9 us
    pallas_call x1, Pallas kernels: 48.3 us -> 48.9 us  [per_device(): pl.pallas_call(functools.partial(fused_kernel, dims), out_shape=jax.Shape...]
where the time goes in v4:
time: 51.2 us; the launch traced here: 50.8 us
  Pallas kernels  48.9 us (96%)
  local copies, waits for them, and re-layouts  1.87 us (4%)
    pallas_call x1, Pallas kernels, per_device(): pl.pallas_call(functools.partial(fused_kernel, dims), out_shape=jax.Shape...  48.9 us
    unnamed x1, local copies, waits for them, and re-layouts  1.87 us

profile of v4, /device:TPU:5, one launch (start us, length us, event | category | flops | bytes accessed | tf_op | source)
XLA Modules:
  0.0 50.8 jit_solution(13397324026133980713)
XLA Ops:
  0.0 48.9 %shard_map.64 = bf16[256,1024]{1,0:T(8,128)(2,1)} custom-call(bf16[3,1024,256]{2,1,0:T(8,128)(2,1)} %proj_hbm.1, f32[3,3,1024]{2,1,0:T(4,128)} %bitcast.6, f32[16,1024]{1,0:T(8,128)} %bitcast.4, f32[16,1024]{1,0:T(8,128)} %bitcast.5, f32[1,1024]{1,0:T(1,128)} %bitcast.7, bf16[4096,1024]{1,0:T(8,128)(2,1)} %w_hbm.1), custom_call_target="tpu_custom_call" | custom-call | flops 2147483648 | bytes 10485760 | tf_op jit(solution)/shard_map/pallas_call | solution.py:586
  48.9 1.9 %copy.8 = bf16[256,1024]{1,0:T(8,128)(2,1)} copy(bf16[256,1024]{1,0:T(8,128)(2,1)} %shard_map.64) | data formatting | bytes 1048576

commit v5 on v4

--- a/solution.py
+++ b/solution.py
@@ -86,7 +86,6 @@
     taps = [[coef(4 * modes + 3 * i + m) for m in range(3)] for i in range(3)]
     skip = coef(4 * modes + 9)
 
-    load_proj.wait()
     row_ids = lax.broadcasted_iota(jnp.int32, (length, length), 0)
     col_ids = lax.broadcasted_iota(jnp.int32, (length, length), 1)
     eye = jnp.where(row_ids == col_ids, 1.0, 0.0).astype(jnp.bfloat16)
@@ -104,9 +103,6 @@
                     turned[:, j * LANES:(j + 1) * LANES]
                 )
 
-    turn(1)
-    turn(2)
-
     pl.semaphore_wait(barrier, n_ctx - 1 + inner)
 
     helped = n_ch == 4 and n_ctx == 8
@@ -121,12 +117,13 @@
             pl.multiple_of(index * piece + which * (piece // 2), piece // 2), piece // 2
         )
 
-    def piece_copy():
+    def piece_copy(which):
+        start = far * width + ctx * piece + which * (piece // 2)
         return pltpu.make_async_remote_copy(
-            src_ref=w_hbm.at[pl.ds(pl.multiple_of(far * width + ctx * piece, piece), piece), :],
-            dst_ref=help_v.at[pl.ds(pl.multiple_of(ctx * piece, piece), piece), :],
-            send_sem=piece_sem.at[0],
-            recv_sem=piece_sem.at[1],
+            src_ref=w_hbm.at[pl.ds(pl.multiple_of(start, piece // 2), piece // 2), :],
+            dst_ref=help_v.at[piece_window(ctx, which), :],
+            send_sem=piece_sem.at[0, which],
+            recv_sem=piece_sem.at[1, which],
             device_id={"ch": jnp.where(ch < n_ch // 2, 1, n_ch - 2)},
             device_id_type=MESH,
         )
@@ -152,21 +149,25 @@
         )
 
     spread_stages = (
-        ((0, ctx, 0), (1, ctx, 1), (2, ctx, 0), (2, ctx, 1)),
-        ((1, ctx, 0), (1, x_peer, 0), (0, ctx, 1), (0, y_peer, 1), (2, x_peer, 0), (2, y_peer, 1)),
+        ((0, ctx, 0), (2, ctx, 0)),
+        ((1, ctx, 1), (2, ctx, 1)),
+        ((1, ctx, 0), (1, x_peer, 0), (2, x_peer, 0)),
+        ((0, ctx, 1), (0, y_peer, 1), (2, y_peer, 1)),
         ((2, y_peer, 0), (2, corner, 0), (2, x_peer, 1), (2, corner, 1)),
     )
     spread_waits = (
         (),
-        ((x_peer, 0), (y_peer, 1)),
+        (),
+        ((x_peer, 0),),
+        ((y_peer, 1),),
         ((y_peer, 0), (corner, 0), (x_peer, 1), (corner, 1)),
     )
 
     def spread_stage(stage):
         @pl.when(inside)
         def _():
-            if stage == 0:
-                piece_copy().wait_recv()
+            if stage < 2:
+                piece_copy(stage).wait_recv()
             for index, which in spread_waits[stage]:
                 spread_copy(0, index, which).wait_recv()
             for way, index, which in spread_stages[stage]:
@@ -175,8 +176,12 @@
     if helped:
         @pl.when(at_end)
         def _():
-            piece_copy().start()
-
+            for which in range(2):
+                piece_copy(which).start()
+
+    load_proj.wait()
+    turn(1)
+    turn(2)
     edge = halo * groups
 
     def halo_copy(first, count):
@@ -357,8 +362,10 @@
         def _():
             block_copy(ch, part, 1).start()
 
+        if helped and part == 0:
+            spread_stage(0)
         if helped and part == 3:
-            spread_stage(0)
+            spread_stage(1)
 
     load_w.wait()
 
@@ -495,12 +502,14 @@
             return carry
 
         if helped and distance == 1:
-            lax.fori_loop(0, parts - 2, one_part, 0)
-            spread_stage(1)
+            lax.fori_loop(0, 2, one_part, 0)
+            spread_stage(2)
+            lax.fori_loop(2, parts - 2, one_part, 0)
+            spread_stage(3)
             lax.fori_loop(parts - 2, parts, one_part, 0)
         elif helped and distance == 2:
             lax.fori_loop(0, cut, one_part, 0)
-            spread_stage(2)
+            spread_stage(4)
             lax.fori_loop(cut, parts - 2, one_part, 0)
             send_partial(0)
             lax.fori_loop(parts - 2, parts, one_part, 0)
@@ -562,7 +571,8 @@
     if helped:
         @pl.when(at_end)
         def _():
-            piece_copy().wait_send()
+            for which in range(2):
+                piece_copy(which).wait_send()
 
         @pl.when(inside)
         def _():
@@ -617,7 +627,7 @@
             pltpu.SemaphoreType.DMA((n_ctx // 2, 2)),
             pltpu.SemaphoreType.DMA((2, n_ch, parts)),
             pltpu.SemaphoreType.DMA((n_ch, parts)),
-            pltpu.SemaphoreType.DMA((2,)),
+            pltpu.SemaphoreType.DMA((2, 2)),
             pltpu.SemaphoreType.DMA((3, n_ctx, 2)),
             pltpu.SemaphoreType.DMA((n_ctx, 2)),
             pltpu.SemaphoreType.DMA((2,)),

time: 51.2 us -> 51.5 us (level)
  the two profiles are of different devices: /device:TPU:5 before, /device:TPU:1 now
where the time goes in v5:
time: 51.5 us; the launch traced here: 51.3 us
  Pallas kernels  49.5 us (96%)
  local copies, waits for them, and re-layouts  1.87 us (4%)
    pallas_call x1, Pallas kernels, per_device(): pl.pallas_call(functools.partial(fused_kernel, dims), out_shape=jax.Shape...  49.5 us
    unnamed x1, local copies, waits for them, and re-layouts  1.87 us

profile of v5, /device:TPU:1, one launch (start us, length us, event | category | flops | bytes accessed | tf_op | source)
XLA Modules:
  0.0 51.3 jit_solution(2798079594202792254)
XLA Ops:
  0.0 49.5 %shard_map.64 = bf16[256,1024]{1,0:T(8,128)(2,1)} custom-call(bf16[3,1024,256]{2,1,0:T(8,128)(2,1)} %proj_hbm.1, f32[3,3,1024]{2,1,0:T(4,128)} %bitcast.6, f32[16,1024]{1,0:T(8,128)} %bitcast.4, f32[16,1024]{1,0:T(8,128)} %bitcast.5, f32[1,1024]{1,0:T(1,128)} %bitcast.7, bf16[4096,1024]{1,0:T(8,128)(2,1)} %w_hbm.1), custom_call_target="tpu_custom_call" | custom-call | flops 2147483648 | bytes 10485760 | tf_op jit(solution)/shard_map/pallas_call | solution.py:596
  49.5 1.9 %copy.8 = bf16[256,1024]{1,0:T(8,128)(2,1)} copy(bf16[256,1024]{1,0:T(8,128)(2,1)} %shard_map.64) | data formatting | bytes 1048576

commit v6 on v5

--- a/solution.py
+++ b/solution.py
@@ -311,6 +311,8 @@
             for m in range(modes)
         )
 
+    if helped:
+        spread_stage(0)
     state = lax.fori_loop(0, chip, take_chip, empty)
     odd = core == 1
     state = tuple(
@@ -363,9 +365,9 @@
             block_copy(ch, part, 1).start()
 
         if helped and part == 0:
-            spread_stage(0)
-        if helped and part == 3:
             spread_stage(1)
+        if helped and part == parts - 1:
+            spread_stage(2)
 
     load_w.wait()
 
@@ -502,11 +504,9 @@
             return carry
 
         if helped and distance == 1:
-            lax.fori_loop(0, 2, one_part, 0)
-            spread_stage(2)
-            lax.fori_loop(2, parts - 2, one_part, 0)
+            lax.fori_loop(0, cut, one_part, 0)
             spread_stage(3)
-            lax.fori_loop(parts - 2, parts, one_part, 0)
+            lax.fori_loop(cut, parts, one_part, 0)
         elif helped and distance == 2:
             lax.fori_loop(0, cut, one_part, 0)
             spread_stage(4)

time: 51.5 us -> 54.4 us (1.056)
  the two profiles are of different devices: /device:TPU:1 before, /device:TPU:0 now
where the time goes in v6:
time: 54.4 us; the launch traced here: 54.2 us
  Pallas kernels  52.3 us (96%)
  local copies, waits for them, and re-layouts  1.87 us (3%)
    pallas_call x1, Pallas kernels, per_device(): pl.pallas_call(functools.partial(fused_kernel, dims), out_shape=jax.Shape...  52.3 us
    unnamed x1, local copies, waits for them, and re-layouts  1.87 us

profile of v6, /device:TPU:0, one launch (start us, length us, event | category | flops | bytes accessed | tf_op | source)
XLA Modules:
  0.0 54.2 jit_solution(13377467959269708861)
XLA Ops:
  0.0 52.3 %shard_map.64 = bf16[256,1024]{1,0:T(8,128)(2,1)} custom-call(bf16[3,1024,256]{2,1,0:T(8,128)(2,1)} %proj_hbm.1, f32[3,3,1024]{2,1,0:T(4,128)} %bitcast.6, f32[16,1024]{1,0:T(8,128)} %bitcast.4, f32[16,1024]{1,0:T(8,128)} %bitcast.5, f32[1,1024]{1,0:T(1,128)} %bitcast.7, bf16[4096,1024]{1,0:T(8,128)(2,1)} %w_hbm.1), custom_call_target="tpu_custom_call" | custom-call | flops 2147483648 | bytes 10485760 | tf_op jit(solution)/shard_map/pallas_call | solution.py:596
  52.4 1.9 %copy.8 = bf16[256,1024]{1,0:T(8,128)(2,1)} copy(bf16[256,1024]{1,0:T(8,128)(2,1)} %shard_map.64) | data formatting | bytes 1048576

commit v7 on v3

--- a/solution.py
+++ b/solution.py
@@ -208,7 +208,7 @@
         )
 
     def send_chip(target, carry):
-        chip_copy(chip, core, target).start()
+        chip_copy(chip, core, n_ctx + 2 * chip + 1 - target).start()
         return carry
 
     lax.fori_loop(2 * chip + 2, n_ctx, send_chip, 0)
@@ -273,7 +273,7 @@
         )
 
     for part in range(parts):
-        state = lax.fori_loop(part * rows, (part + 1) * rows, finish, state, unroll=4)
+        state = lax.fori_loop(part * rows, (part + 1) * rows, finish, state, unroll=8)
         for group in range(groups):
             tile = gate_rows[pl.ds(part * rows * groups + group, rows, stride=groups), :]
             gathered[ch, part * rows:(part + 1) * rows, group * LANES:(group + 1) * LANES] = (

time: 50.5 us -> 50.4 us (level); the launches traced: 50.2 us -> 49.6 us
  Pallas kernels: 48.3 us -> 47.7 us
    pallas_call x1, Pallas kernels: 48.3 us -> 47.7 us  [per_device(): pl.pallas_call(functools.partial(fused_kernel, dims), out_shape=jax.Shape...]
where the time goes in v7:
time: 50.4 us; the launch traced here: 49.6 us
  Pallas kernels  47.7 us (95%)
  local copies, waits for them, and re-layouts  1.87 us (4%)
    pallas_call x1, Pallas kernels, per_device(): pl.pallas_call(functools.partial(fused_kernel, dims), out_shape=jax.Shape...  47.7 us
    unnamed x1, local copies, waits for them, and re-layouts  1.87 us

profile of v7, /device:TPU:5, one launch (start us, length us, event | category | flops | bytes accessed | tf_op | source)
XLA Modules:
  0.0 49.6 jit_solution(1385818693430378155)
XLA Ops:
  0.0 47.7 %shard_map.64 = bf16[256,1024]{1,0:T(8,128)(2,1)} custom-call(bf16[3,1024,256]{2,1,0:T(8,128)(2,1)} %proj_hbm.1, f32[3,3,1024]{2,1,0:T(4,128)} %bitcast.6, f32[16,1024]{1,0:T(8,128)} %bitcast.4, f32[16,1024]{1,0:T(8,128)} %bitcast.5, f32[1,1024]{1,0:T(1,128)} %bitcast.7, bf16[4096,1024]{1,0:T(8,128)(2,1)} %w_hbm.1), custom_call_target="tpu_custom_call" | custom-call | flops 2147483648 | bytes 10485760 | tf_op jit(solution)/shard_map/pallas_call | solution.py:422
  47.7 1.9 %copy.8 = bf16[256,1024]{1,0:T(8,128)(2,1)} copy(bf16[256,1024]{1,0:T(8,128)(2,1)} %shard_map.64) | data formatting | bytes 1048576
